TPU v7x, 32 devices: a whole 2x2x4 slice. The times are simulated.
32 devices in a mesh: grp: 2 (over x), seg: 16 (over z, y, core).
Axes of the slice: x: 2, y: 2, z: 4, core: 2. Of those that a mesh axis runs over, the one named last changes fastest.
Arguments:
- strain: float32 [2097152], P(('grp', 'seg')), parts along dimension 0, may hold values from -6 to 6
- gate_mask: int32 [2097152], P(('grp', 'seg')), parts along dimension 0, may hold values 0 or 1
- template_bank: bfloat16 [32, 2, 32768], P('grp', None, 'seg'), parts along dimension 0, may hold values from -6 to 6
Outputs:
- peak_power: float32 [16, 8192], P(None, ('grp', 'seg')), parts along dimension 1
There are 2 independent parts, one for each index of `grp`. A program takes and returns all parts, laid end to end along the dimension named above; each array names one. Nothing has to cross between parts.
All inputs are finite; a program needn't handle non-finite values. No bound on the sum of `gate_mask` on one device may be relied on, other than what follows from the above.
Results may differ from a plain program's by a relative error of at most 0.0003.
Values may be sent and summed in bfloat16 or wider, within the bound.
A program may use at most 128 MiB of HBM per device.

v0:
```python
import functools
import math

import jax
import jax.numpy as jnp
import ml_dtypes
import numpy as np
from jax import lax
from jax.experimental import pallas as pl
from jax.experimental.pallas import tpu as pltpu
from jax.sharding import PartitionSpec as P

RADIX = 256
HALF = RADIX // 2
BLOCK = 32768
EPSILON = 1e-06
BF16 = jnp.bfloat16
F32 = jnp.float32
VMEM_LIMIT = 48 * 1024 * 1024


def angles(rows, cols, period):
    phase = np.outer(np.arange(rows), np.arange(cols)) % period
    turn = phase * (2.0 * math.pi / period)
    return np.cos(turn), np.sin(turn)


def two_parts(table):
    high = table.astype(ml_dtypes.bfloat16)
    low = (table - high.astype(np.float64)).astype(ml_dtypes.bfloat16)
    return high, low


@functools.cache
def forward_tables():
    cos, sin = angles(HALF, RADIX, RADIX)
    first = np.concatenate([cos, -sin], axis=1)
    cos, sin = angles(RADIX, RADIX, RADIX * RADIX)
    twist = np.stack([cos, -sin]).astype(np.float32)
    cos, sin = angles(HALF, RADIX, RADIX)
    second = np.block([[cos, sin], [-sin, cos]])
    return two_parts(first) + (twist,) + two_parts(second)


@functools.cache
def inverse_tables():
    cos, sin = angles(RADIX, HALF, RADIX)
    first = np.block([[cos, -sin], [sin, cos]])
    cos, sin = angles(RADIX, RADIX, RADIX * RADIX)
    twist = np.stack([cos, sin]).astype(np.float32)
    cos, sin = angles(RADIX, HALF, RADIX)
    second = np.block([[cos, sin], [-sin, cos]])
    return two_parts(first) + (twist,) + two_parts(second)


def split(value):
    high = value.astype(BF16)
    return high, (value - high.astype(F32)).astype(BF16)


def dot(left, right):
    return jnp.dot(left, right, preferred_element_type=F32)


def forward_kernel(g_ref, prev_ref, th_ref, tl_ref, w_ref, uh_ref, ul_ref, x_ref):
    def grid_of(ref, block):
        halves = [ref[pl.ds(block * RADIX + half, HALF, stride=2), :] for half in range(2)]
        return jnp.concatenate([half.T for half in halves], axis=0)

    def first_stage(grid):
        high, low = split(grid)
        return dot(high, th_ref[...]) + dot(low, th_ref[...]) + dot(high, tl_ref[...])

    parity = lax.broadcasted_iota(jnp.int32, (RADIX, 2 * RADIX), 1) % 2
    sign = (1 - 2 * parity).astype(F32)
    blocks = [first_stage(grid_of(prev_ref, 0))]
    blocks += [first_stage(grid_of(g_ref, block)) for block in range(2)]
    for block in range(2):
        both = blocks[block + 1] + sign * blocks[block]
        real, imag = both[:, :RADIX], both[:, RADIX:]
        cos, sin = w_ref[0], w_ref[1]
        turned = jnp.concatenate([real * cos - imag * sin, real * sin + imag * cos], axis=0)
        high, low = split(turned)
        x_ref[block] = dot(uh_ref[...], high) + dot(uh_ref[...], low) + dot(ul_ref[...], high)


def inverse_kernel(h_ref, x_ref, th_ref, tl_ref, w_ref, uh_ref, ul_ref, o_ref):
    index = pl.program_id(0)
    bank_real = h_ref[0, 0].astype(F32)
    bank_imag = h_ref[0, 1].astype(F32)
    power_sum = jnp.sum(bank_real * bank_real + bank_imag * bank_imag)
    scale = 1.0 / (BLOCK * power_sum + EPSILON)
    cos, sin = w_ref[0], w_ref[1]
    peaks = []
    for block in range(2):
        real, imag = x_ref[block, :HALF], x_ref[block, HALF:]
        product = jnp.concatenate(
            [real * bank_real + imag * bank_imag, imag * bank_real - real * bank_imag], axis=0
        )
        high, low = split(product)
        part = dot(th_ref[...], high) + dot(tl_ref[...], high) + dot(th_ref[...], low)
        real, imag = part[:RADIX], part[RADIX:]
        turned = jnp.concatenate([real * cos - imag * sin, real * sin + imag * cos], axis=1)
        high, low = split(turned)
        series = dot(high, uh_ref[...]) + dot(low, uh_ref[...]) + dot(high, ul_ref[...])
        real, imag = series[:, :HALF], series[:, HALF:]
        peaks.append(jnp.max(real * real + imag * imag, axis=0, keepdims=True))
    row = lax.broadcasted_iota(jnp.int32, o_ref.shape, 0)
    o_ref[...] = jnp.where(row == index, jnp.concatenate(peaks, axis=1) * scale, o_ref[...])


def whole(shape):
    return pl.BlockSpec(shape, lambda *_: (0,) * len(shape))


def local(strain, gate_mask, template_bank):
    template_total = template_bank.shape[0]
    gated = (strain * gate_mask.astype(F32)).reshape(-1, 128)
    count = lax.axis_size("seg")
    pairs = [(i, i + 1) for i in range(count - 1)]
    prev = lax.ppermute(gated[-RADIX:], "seg", pairs)
    rows = template_bank.reshape(template_total, 2, -1, RADIX)
    bank = lax.all_gather(rows, "seg", axis=2, tiled=True)
    spectra = pl.pallas_call(
        forward_kernel,
        out_shape=jax.ShapeDtypeStruct((2, RADIX, RADIX), F32),
        compiler_params=pltpu.CompilerParams(vmem_limit_bytes=VMEM_LIMIT),
        cost_estimate=pl.CostEstimate(flops=6 * 120_000_000, bytes_accessed=3_000_000, transcendentals=0),
        name="window_spectra",
    )(gated, prev, *(jnp.asarray(t) for t in forward_tables()))
    tables = [jnp.asarray(t) for t in inverse_tables()]
    return pl.pallas_call(
        inverse_kernel,
        out_shape=jax.ShapeDtypeStruct((template_total, RADIX), F32),
        grid=(template_total,),
        in_specs=[
            pl.BlockSpec((1, 2, HALF, RADIX), lambda k: (k, 0, 0, 0)),
            whole((2, RADIX, RADIX)),
            *(whole(t.shape) for t in tables),
        ],
        out_specs=whole((template_total, RADIX)),
        compiler_params=pltpu.CompilerParams(vmem_limit_bytes=VMEM_LIMIT),
        name="series_peaks",
    )(bank, spectra, *tables)


def solution(mesh):
    in_specs = (P(("grp", "seg")), P(("grp", "seg")), P("grp", None, "seg"))
    out_specs = P(None, ("grp", "seg"))
    return jax.shard_map(local, mesh=mesh, in_specs=in_specs, out_specs=out_specs, check_vma=False)
```

profile of v0, /device:TPU:0, one launch (start us, length us, event | category | flops | bytes accessed | tf_op | source)
XLA Modules:
  0.0 87.5 jit_solution(7986155912278112103)
XLA Ops:
  6.5 0.0 copy-start.2
  6.5 0.0 copy-start.3
  6.5 0.0 copy-start.1
  6.5 0.0 copy-start.4
  6.5 0.0 copy-start.5
  6.6 0.0 all-gather.2.cloned.1.call-start
  6.6 1.7 %reshape.15 = bf16[16,2,8,256]{3,2,1,0:T(8,128)(2,1)} reshape(bf16[16,2,2048]{2,1,0:T(2,128)(2,1)} %param.15) | data formatting | bytes 262144 | tf_op jit(solution)/shard_map/reshape | solution.py:122
  8.3 0.0 all-gather.2.cloned.1.call-update
  8.4 1.1 %convert_multiply_fusion = f32[65536]{0:T(1024)S(1)} fusion(f32[65536]{0:T(1024)} %param.13, s32[65536]{0:T(1024)} %param.14), kind=kLoop, calls=%fused_computation | loop fusion | flops 131072 | bytes 786432 | tf_op jit(solution)/shard_map/mul | solution.py:118
  9.4 2.4 %collective-permute-start = (f32[256,128]{1,0:T(8,128)S(1)}, f32[256,128]{1,0:T(8,128)S(1)}, u32[]{:S(2)}, u32[]{:S(2)}) collective-permute-start(f32[256,128]{1,0:T(8,128)S(1)} %slice_bitcast_fusion), channel_id=1, source_target_pairs={{0,1},{1,2},{2,3},{3,4},{4,5},{5,6},{6,7},{7,8},{8,9},{9,10},{10,1... | collective-permute-start | bytes 393224 | tf_op jit(solution)/shard_map/ppermute | solution.py:121
  11.8 1.0 %collective-permute-done.prev_ref = f32[256,128]{1,0:T(8,128)S(1)} collective-permute-done((f32[256,128]{1,0:T(8,128)S(1)}, f32[256,128]{1,0:T(8,128)S(1)}, u32[]{:S(2)}, u32[]{:S(2)}) %collective-permute-start) | collective-permute-done | bytes 131104 | tf_op jit(solution)/shard_map/ppermute | solution.py:121
  12.8 0.0 copy-start.6
  12.8 1.0 %copy-done.6 = f32[2,256,256]{2,1,0:T(8,128)S(1)} copy-done((f32[2,256,256]{2,1,0:T(8,128)S(1)}, f32[2,256,256]{2,1,0:T(8,128)}, u32[]{:S(2)}) %copy-start.6) | copy-done | bytes 524312
  13.8 0.0 copy-start.7
  13.8 0.9 %copy-done.7 = bf16[256,512]{1,0:T(8,128)(2,1)S(1)} copy-done((bf16[256,512]{1,0:T(8,128)(2,1)S(1)}, bf16[256,512]{1,0:T(8,128)(2,1)}, u32[]{:S(2)}) %copy-start.7) | copy-done | bytes 262168
  14.8 0.0 copy-start.8
  14.8 0.9 %copy-done.8 = bf16[256,512]{1,0:T(8,128)(2,1)S(1)} copy-done((bf16[256,512]{1,0:T(8,128)(2,1)S(1)}, bf16[256,512]{1,0:T(8,128)(2,1)}, u32[]{:S(2)}) %copy-start.8) | copy-done | bytes 262168
  15.7 0.0 copy-start.9
  15.7 0.9 %copy-done.9 = bf16[128,512]{1,0:T(8,128)(2,1)S(1)} copy-done((bf16[128,512]{1,0:T(8,128)(2,1)S(1)}, bf16[128,512]{1,0:T(8,128)(2,1)}, u32[]{:S(2)}) %copy-start.9) | copy-done | bytes 131096
  16.6 0.0 copy-start.10
  16.6 0.9 %copy-done.10 = bf16[128,512]{1,0:T(8,128)(2,1)S(1)} copy-done((bf16[128,512]{1,0:T(8,128)(2,1)S(1)}, bf16[128,512]{1,0:T(8,128)(2,1)}, u32[]{:S(2)}) %copy-start.10) | copy-done | bytes 131096
  17.5 1.4 %window_spectra.1.x_ref = f32[2,256,256]{2,1,0:T(8,128)S(1)} custom-call(f32[512,128]{1,0:T(8,128)S(1)} %bitcast.3, f32[256,128]{1,0:T(8,128)S(1)} %collective-permute-done.prev_ref, bf16[128,512]{1,0:T(8,128)(2,1)S(1)} %copy-done.9, bf16[128,512]{1,0:T(8,128)(2,1)S(1)} %copy-done.10, f32[2,256,256]{2,1,0:T(8,128)S(1)} %copy-done.6, ...), custom_call_target="tpu_custom_call" | custom-call | flops 720000000 | bytes 3000000 | tf_op jit(solution)/shard_map/window_spectra/pallas_call | solution.py:124
  19.0 34.5 %all-gather.2.cloned.1.call-done.h_ref = bf16[16,2,128,256]{3,2,1,0:T(8,128)(2,1)} async-done(((bf16[16,2,8,256]{3,2,1,0:T(8,128)(2,1)}), bf16[16,2,128,256]{3,2,1,0:T(8,128)(2,1)}) %all-gather.2.cloned.1.call-update) | async-done | bytes 2097168 | tf_op jit(solution)/shard_map/all_gather | solution.py:123
  53.5 0.0 copy-done.2
  53.5 0.0 copy-done.3
  53.5 0.0 copy-done.1
  53.5 0.0 copy-done.4
  53.5 0.0 copy-done.5
  53.5 0.0 copy-start
  53.5 1.6 %copy-done = bf16[16,2,128,256]{3,2,1,0:T(8,128)(2,1)S(1)} copy-done((bf16[16,2,128,256]{3,2,1,0:T(8,128)(2,1)S(1)}, bf16[16,2,128,256]{3,2,1,0:T(8,128)(2,1)}, u32[]{:S(2)}) %copy-start) | copy-done | bytes 2097176
  55.1 25.6 %series_peaks.1 = f32[16,256]{1,0:T(8,128)} custom-call(bf16[16,2,128,256]{3,2,1,0:T(8,128)(2,1)S(1)} %copy-done, f32[2,256,256]{2,1,0:T(8,128)S(1)} %window_spectra.1.x_ref, bf16[512,256]{1,0:T(8,128)(2,1)S(1)} %copy-done.2, bf16[512,256]{1,0:T(8,128)(2,1)S(1)} %copy-done.3, f32[2,256,256]{2,1,0:T(8,128)S(1)} %copy-done.1, bf16[512,256]{1,0:T(8,128)(2,1)S(1)} %copy-done.4, ...), custom_call_target="tpu_custom_call" | custom-call | tf_op jit(solution)/shard_map/series_peaks/pallas_call | solution.py:132
  (1 shorter events, 0.0 us)
Async XLA Ops:
  6.5 47.0 %copy-start.2 = (bf16[512,256]{1,0:T(8,128)(2,1)S(1)}, bf16[512,256]{1,0:T(8,128)(2,1)}, u32[]{:S(2)}) copy-start(bf16[512,256]{1,0:T(8,128)(2,1)} %constant.25.clone.th_ref) | copy-start | bytes 786436
  6.5 47.0 %copy-start.3 = (bf16[512,256]{1,0:T(8,128)(2,1)S(1)}, bf16[512,256]{1,0:T(8,128)(2,1)}, u32[]{:S(2)}) copy-start(bf16[512,256]{1,0:T(8,128)(2,1)} %constant.26.clone.tl_ref) | copy-start | bytes 786436
  6.5 47.0 %copy-start.1 = (f32[2,256,256]{2,1,0:T(8,128)S(1)}, f32[2,256,256]{2,1,0:T(8,128)}, u32[]{:S(2)}) copy-start(f32[2,256,256]{2,1,0:T(8,128)} %constant.27.clone.w_ref) | copy-start | bytes 1572868
  6.5 47.0 %copy-start.4 = (bf16[512,256]{1,0:T(8,128)(2,1)S(1)}, bf16[512,256]{1,0:T(8,128)(2,1)}, u32[]{:S(2)}) copy-start(bf16[512,256]{1,0:T(8,128)(2,1)} %constant.28.clone.uh_ref) | copy-start | bytes 786436
  6.5 47.0 %copy-start.5 = (bf16[512,256]{1,0:T(8,128)(2,1)S(1)}, bf16[512,256]{1,0:T(8,128)(2,1)}, u32[]{:S(2)}) copy-start(bf16[512,256]{1,0:T(8,128)(2,1)} %constant.29.clone.ul_ref) | copy-start | bytes 786436
  6.6 46.9 %all-gather.2.cloned.1.call-start = ((), (), s32[]{:S(2)}) async-start(), calls=%async_computation | async-start | bytes 2228224 | tf_op jit(solution)/shard_map/all_gather | solution.py:123
  9.4 3.3 %collective-permute-start = (f32[256,128]{1,0:T(8,128)S(1)}, f32[256,128]{1,0:T(8,128)S(1)}, u32[]{:S(2)}, u32[]{:S(2)}) collective-permute-start(f32[256,128]{1,0:T(8,128)S(1)} %slice_bitcast_fusion), channel_id=1, source_target_pairs={{0,1},{1,2},{2,3},{3,4},{4,5},{5,6},{6,7},{7,8},{8,9},{9,10},{10,1... | collective-permute-start | bytes 393224 | tf_op jit(solution)/shard_map/ppermute | solution.py:121
  12.8 1.0 %copy-start.6 = (f32[2,256,256]{2,1,0:T(8,128)S(1)}, f32[2,256,256]{2,1,0:T(8,128)}, u32[]{:S(2)}) copy-start(f32[2,256,256]{2,1,0:T(8,128)} %constant.22.clone.w_ref) | copy-start | bytes 1572868
  13.8 0.9 %copy-start.7 = (bf16[256,512]{1,0:T(8,128)(2,1)S(1)}, bf16[256,512]{1,0:T(8,128)(2,1)}, u32[]{:S(2)}) copy-start(bf16[256,512]{1,0:T(8,128)(2,1)} %constant.23.clone.uh_ref) | copy-start | bytes 786436
  14.8 0.9 %copy-start.8 = (bf16[256,512]{1,0:T(8,128)(2,1)S(1)}, bf16[256,512]{1,0:T(8,128)(2,1)}, u32[]{:S(2)}) copy-start(bf16[256,512]{1,0:T(8,128)(2,1)} %constant.24.clone.ul_ref) | copy-start | bytes 786436
  15.7 0.9 %copy-start.9 = (bf16[128,512]{1,0:T(8,128)(2,1)S(1)}, bf16[128,512]{1,0:T(8,128)(2,1)}, u32[]{:S(2)}) copy-start(bf16[128,512]{1,0:T(8,128)(2,1)} %constant.20.clone.th_ref) | copy-start | bytes 393220
  16.6 0.9 %copy-start.10 = (bf16[128,512]{1,0:T(8,128)(2,1)S(1)}, bf16[128,512]{1,0:T(8,128)(2,1)}, u32[]{:S(2)}) copy-start(bf16[128,512]{1,0:T(8,128)(2,1)} %constant.21.clone.tl_ref) | copy-start | bytes 393220
  53.5 1.6 %copy-start = (bf16[16,2,128,256]{3,2,1,0:T(8,128)(2,1)S(1)}, bf16[16,2,128,256]{3,2,1,0:T(8,128)(2,1)}, u32[]{:S(2)}) copy-start(bf16[16,2,128,256]{3,2,1,0:T(8,128)(2,1)} %all-gather.2.cloned.1.call-done.h_ref) | copy-start | bytes 6291460
Sparse Core Ops, SparseCore 0:
  9.5 43.9 all-gather.1
where the time goes:
time: 87.9 us; the launch traced here: 87.5 us
  waiting for transfers between devices  35.5 us (40%)
  Pallas kernels  27 us (31%)
  between operations  13.5 us (15%)
  local copies, waits for them, and re-layouts  8.11 us (9%)
  starting transfers between devices  2.4 us (3%)
  other arithmetic  1.06 us (1%)
    all_gather x1, waiting for transfers between devices, local(): bank = lax.all_gather(rows, 'seg', axis=2, tiled=True)  34.5 us
    pallas_call x1, Pallas kernels, local(): pl.pallas_call(inverse_kernel, out_shape=jax.ShapeDtypeStruct((template_t...  25.6 us
    unnamed x22, local copies, waits for them, and re-layouts  6.35 us
    ppermute x1, starting transfers between devices, local(): prev = lax.ppermute(gated[-RADIX:], 'seg', pairs)  2.36 us
  transfers between devices with their start and end apart: 2, of which 2 were waited for; matrix products, arithmetic and copies ran while one was open for 1% of the time, Pallas kernels for 2%

commit v1 on v0

v1 whole, which is shorter than its diff:
```python
import functools
import math

import jax
import jax.numpy as jnp
import ml_dtypes
import numpy as np
from jax import lax
from jax.experimental import pallas as pl
from jax.experimental.pallas import tpu as pltpu
from jax.sharding import PartitionSpec as P

RADIX = 256
HALF = RADIX // 2
BLOCK = 32768
EPSILON = 1e-06
BF16 = jnp.bfloat16
F32 = jnp.float32
MESH = pl.DeviceIdType.MESH
VMEM_LIMIT = 56 * 1024 * 1024
SEGS = 16
GROUP = 2
GROUPS = 8


def angles(rows, cols, period):
    phase = np.outer(np.arange(rows), np.arange(cols)) % period
    turn = phase * (2.0 * math.pi / period)
    return np.cos(turn), np.sin(turn)


def two_parts(table):
    high = table.astype(ml_dtypes.bfloat16)
    low = (table - high.astype(np.float64)).astype(ml_dtypes.bfloat16)
    return high, low


@functools.cache
def forward_tables():
    cos, sin = angles(HALF, RADIX, RADIX)
    high, low = two_parts(np.concatenate([cos, -sin], axis=1))
    cos, sin = angles(HALF, RADIX, RADIX)
    second = two_parts(np.block([[cos, sin], [-sin, cos]]))
    return high, low, np.concatenate([second[0], second[1], second[0]], axis=1)


@functools.cache
def inverse_tables():
    cos, sin = angles(RADIX, HALF, RADIX)
    first = two_parts(np.block([[cos, -sin], [sin, cos]]))
    cos, sin = angles(RADIX, RADIX, RADIX * RADIX)
    twist = np.stack([cos, sin]).astype(np.float32)
    cos, sin = angles(RADIX, HALF, RADIX)
    second = two_parts(np.block([[cos, sin], [-sin, cos]]))
    return (
        np.concatenate([first[0], first[1], first[0]], axis=1),
        twist,
        np.concatenate([second[0], second[0], second[1]], axis=0),
    )


def split(value):
    high = value.astype(BF16)
    return high, (value - high.astype(F32)).astype(BF16)


def dot(left, right):
    return jnp.dot(left, right, preferred_element_type=F32)


def inverse_kernel(h_ref, x_ref, t_ref, w_ref, u_ref, o_ref):
    index = pl.program_id(0)
    peaks = template_peaks([(h_ref[0, 0], h_ref[0, 1])], x_ref, t_ref, w_ref, u_ref)[0]
    row = lax.broadcasted_iota(jnp.int32, o_ref.shape, 0)
    o_ref[...] = jnp.where(row == index, peaks, o_ref[...])


def template_peaks(banks, x_ref, t_ref, w_ref, u_ref):
    wide = [(real.astype(F32), imag.astype(F32)) for real, imag in banks]
    scales = [
        1.0 / (BLOCK * jnp.sum(real * real + imag * imag) + EPSILON) for real, imag in wide
    ]

    def first(item):
        bank_real, bank_imag = wide[item // 2]
        real, imag = x_ref[item % 2, :HALF], x_ref[item % 2, HALF:]
        high, low = split(
            jnp.concatenate(
                [real * bank_real + imag * bank_imag, imag * bank_real - real * bank_imag], axis=0
            )
        )
        return dot(t_ref[...], jnp.concatenate([high, high, low], axis=0))

    def second(part):
        real, imag = part[:RADIX], part[RADIX:]
        cos, sin = w_ref[0], w_ref[1]
        high, low = split(
            jnp.concatenate([real * cos - imag * sin, real * sin + imag * cos], axis=1)
        )
        return dot(jnp.concatenate([high, low, high], axis=1), u_ref[...])

    def peak(series):
        real, imag = series[:, :HALF], series[:, HALF:]
        return jnp.max(real * real + imag * imag, axis=0, keepdims=True)

    count = 2 * len(banks)
    parts = [first(0)]
    peaks = []
    for item in range(count):
        if item + 1 < count:
            parts.append(first(item + 1))
        peaks.append(peak(second(parts[item])))
    return [
        jnp.concatenate(peaks[2 * i : 2 * i + 2], axis=1) * scales[i] for i in range(len(banks))
    ]


def window_spectra(grids, th_ref, tl_ref, w_ref, u_ref, x_ref):
    def first_stage(grid):
        high, low = split(grid)
        return dot(high, th_ref[...]) + dot(low, th_ref[...]) + dot(high, tl_ref[...])

    parity = lax.broadcasted_iota(jnp.int32, (RADIX, 2 * RADIX), 1) % 2
    sign = (1 - 2 * parity).astype(F32)
    blocks = [first_stage(grid) for grid in grids]
    for block in range(2):
        both = blocks[block + 1] + sign * blocks[block]
        real, imag = both[:, :RADIX], both[:, RADIX:]
        cos, sin = w_ref[0], w_ref[1]
        high, low = split(
            jnp.concatenate([real * cos + imag * sin, imag * cos - real * sin], axis=0)
        )
        x_ref[block] = dot(u_ref[...], jnp.concatenate([high, high, low], axis=0))


def grid_of(ref, start):
    halves = [ref[pl.ds(start + half, HALF, stride=2), :] for half in range(2)]
    return jnp.concatenate([half.T for half in halves], axis=0)


def forward_kernel(g_ref, prev_ref, th_ref, tl_ref, w_ref, u_ref, x_ref):
    grids = [grid_of(prev_ref, 0), grid_of(g_ref, 0), grid_of(g_ref, RADIX)]
    window_spectra(grids, th_ref, tl_ref, w_ref, u_ref, x_ref)


def fused_kernel(
    strain_ref, mask_ref, bank_ref, th_ref, tl_ref, w_ref, fu_ref, t_ref, u_ref, o_ref,
    gated, prev, held, x_ref, prev_sem, own_send, pass_send, recv_sem,
):
    me = lax.axis_index("seg")
    z_peers = [(me + 4 * step) % SEGS for step in range(1, 4)]
    y_peer = me + 2 - 4 * ((me // 2) % 2)
    sibling = me + 1 - 2 * (me % 2)
    last = SEGS - 1

    barrier = pltpu.get_barrier_semaphore()
    for peer in (*z_peers, y_peer, sibling, (me + last) % SEGS):
        pl.semaphore_signal(barrier, inc=1, device_id={"seg": peer}, device_id_type=MESH)

    gated[...] = strain_ref[...] * mask_ref[...].astype(F32)
    held[me] = bank_ref[...]

    pl.semaphore_wait(barrier, 6)

    def prev_copy():
        return pltpu.make_async_remote_copy(
            src_ref=gated.at[pl.ds(RADIX, RADIX)],
            dst_ref=prev,
            send_sem=prev_sem.at[0],
            recv_sem=prev_sem.at[1],
            device_id={"seg": me + 1},
            device_id_type=MESH,
        )

    @pl.when(me < last)
    def _():
        prev_copy().start()

    def chunk_copy(group, chunk, send_sem, peer):
        piece = held.at[chunk, pl.ds(group * GROUP, GROUP)]
        return pltpu.make_async_remote_copy(
            src_ref=piece,
            dst_ref=piece,
            send_sem=send_sem,
            recv_sem=recv_sem.at[group, chunk],
            device_id={"seg": peer},
            device_id_type=MESH,
        )

    def own_copies(group):
        return [
            chunk_copy(group, me, own_send.at[group, i], peer)
            for i, peer in enumerate((*z_peers, y_peer, sibling))
        ]

    def z_chunks():
        return z_peers

    def y_chunks():
        return [(y_peer + 4 * step) % SEGS for step in range(4)]

    def sibling_chunks():
        mine = [(me + 4 * step) % SEGS for step in range(4)] + y_chunks()
        return [chunk + 1 - 2 * (chunk % 2) for chunk in mine]

    def z_copies(group):
        return [
            chunk_copy(group, chunk, pass_send.at[group, 2 * i + j], peer)
            for i, chunk in enumerate(z_chunks())
            for j, peer in enumerate((y_peer, sibling))
        ]

    def y_copies(group):
        return [
            chunk_copy(group, chunk, pass_send.at[group, 6 + i], sibling)
            for i, chunk in enumerate(y_chunks())
        ]

    def arrived(group, chunk):
        chunk_copy(group, chunk, own_send.at[group, 0], sibling).wait_recv()

    def pass_z(group):
        copies = z_copies(group)
        for i, chunk in enumerate(z_chunks()):
            arrived(group, chunk)
            copies[2 * i].start()
            copies[2 * i + 1].start()

    def pass_y(group):
        copies = y_copies(group)
        for i, chunk in enumerate(y_chunks()):
            arrived(group, chunk)
            copies[i].start()

    def start_own(group, carry):
        for copy in own_copies(group):
            copy.start()
        return carry

    lax.fori_loop(0, GROUPS, start_own, 0)
    o_ref[...] = jnp.zeros_like(o_ref)

    @pl.when(me == 0)
    def _():
        prev[...] = jnp.zeros_like(prev)

    pass_z(0)

    @pl.when(me > 0)
    def _():
        prev_copy().wait_recv()

    pass_z(1)
    grids = [grid_of(prev, 0), grid_of(gated, 0), grid_of(gated, RADIX)]
    window_spectra(grids, th_ref, tl_ref, w_ref, fu_ref, x_ref)
    pass_y(0)

    def step(group, carry):
        @pl.when(group + 2 < GROUPS)
        def _():
            pass_z(group + 2)

        @pl.when(group + 1 < GROUPS)
        def _():
            pass_y(group + 1)

        for chunk in sibling_chunks():
            arrived(group, chunk)
        banks = []
        for item in range(GROUP):
            rows = held[:, group * GROUP + item]
            banks.append(
                (rows[:, : rows.shape[1] // 2], rows[:, rows.shape[1] // 2 :])
            )
        banks = [
            (real.astype(F32).reshape(HALF, RADIX), imag.astype(F32).reshape(HALF, RADIX))
            for real, imag in banks
        ]
        row = lax.broadcasted_iota(jnp.int32, o_ref.shape, 0)
        total = o_ref[...]
        for item, peaks in enumerate(template_peaks(banks, x_ref, t_ref, w_ref, u_ref)):
            total = jnp.where(row == group * GROUP + item, peaks, total)
        o_ref[...] = total
        return carry

    lax.fori_loop(0, GROUPS, step, 0)

    def finish(group, carry):
        for copy in own_copies(group) + z_copies(group) + y_copies(group):
            copy.wait_send()
        return carry

    lax.fori_loop(0, GROUPS, finish, 0)

    @pl.when(me < last)
    def _():
        prev_copy().wait_send()


def fused(strain, gate_mask, rows):
    template_total = rows.shape[0]
    th, tl, fu = (jnp.asarray(t) for t in forward_tables())
    t3, twist, u3 = (jnp.asarray(t) for t in inverse_tables())
    vmem = pl.BlockSpec(memory_space=pltpu.VMEM)
    return pl.pallas_call(
        fused_kernel,
        out_shape=jax.ShapeDtypeStruct((template_total, RADIX), F32),
        in_specs=[vmem] * 9,
        out_specs=vmem,
        scratch_shapes=[
            pltpu.VMEM((2 * RADIX, 128), F32),
            pltpu.VMEM((RADIX, 128), F32),
            pltpu.VMEM((SEGS, *rows.shape), BF16),
            pltpu.VMEM((2, RADIX, RADIX), F32),
            pltpu.SemaphoreType.DMA((2,)),
            pltpu.SemaphoreType.DMA((GROUPS, 5)),
            pltpu.SemaphoreType.DMA((GROUPS, 10)),
            pltpu.SemaphoreType.DMA((GROUPS, SEGS)),
        ],
        compiler_params=pltpu.CompilerParams(
            vmem_limit_bytes=VMEM_LIMIT, collective_id=0, has_side_effects=True
        ),
        name="matched_filter",
    )(strain.reshape(-1, 128), gate_mask.reshape(-1, 128), rows, th, tl, twist, fu, t3, u3)


def whole(shape):
    return pl.BlockSpec(shape, lambda *_: (0,) * len(shape))


def local(strain, gate_mask, template_bank):
    template_total = template_bank.shape[0]
    count = lax.axis_size("seg")
    if count == SEGS and template_total == GROUP * GROUPS:
        return fused(strain, gate_mask, template_bank.reshape(template_total, -1, RADIX))
    gated = (strain * gate_mask.astype(F32)).reshape(-1, 128)
    pairs = [(i, i + 1) for i in range(count - 1)]
    prev = lax.ppermute(gated[-RADIX:], "seg", pairs)
    rows = template_bank.reshape(template_total, 2, -1, RADIX)
    bank = lax.all_gather(rows, "seg", axis=2, tiled=True)
    th, tl, fu = (jnp.asarray(t) for t in forward_tables())
    t3, twist, u3 = (jnp.asarray(t) for t in inverse_tables())
    params = pltpu.CompilerParams(vmem_limit_bytes=VMEM_LIMIT)
    spectra = pl.pallas_call(
        forward_kernel,
        out_shape=jax.ShapeDtypeStruct((2, RADIX, RADIX), F32),
        compiler_params=params,
        name="window_spectra",
    )(gated, prev, th, tl, twist, fu)
    tables = (t3, twist, u3)
    return pl.pallas_call(
        inverse_kernel,
        out_shape=jax.ShapeDtypeStruct((template_total, RADIX), F32),
        grid=(template_total,),
        in_specs=[
            pl.BlockSpec((1, 2, HALF, RADIX), lambda k: (k, 0, 0, 0)),
            whole((2, RADIX, RADIX)),
            *(whole(t.shape) for t in tables),
        ],
        out_specs=whole((template_total, RADIX)),
        compiler_params=params,
        name="series_peaks",
    )(bank, spectra, *tables)


def solution(mesh):
    in_specs = (P(("grp", "seg")), P(("grp", "seg")), P("grp", None, "seg"))
    out_specs = P(None, ("grp", "seg"))
    return jax.shard_map(local, mesh=mesh, in_specs=in_specs, out_specs=out_specs, check_vma=False)
```

time: 87.9 us -> 41.9 us (0.48)
  waiting for transfers between devices: 35.5 us -> 0 us
  between operations: 13.5 us -> 0.01 us
  Pallas kernels: 27 us -> 38.7 us
  local copies, waits for them, and re-layouts: 8.11 us -> 2.95 us
  starting transfers between devices: 2.4 us -> 0 us
  other arithmetic: 1.06 us -> 0 us
    all_gather x1 -> x0, waiting for transfers between devices: 34.5 us -> none  [local(): bank = lax.all_gather(rows, 'seg', axis=2, tiled=True)]
    pallas_call x2 -> x1, Pallas kernels: 27 us -> 38.7 us  [fused(): pl.pallas_call(fused_kernel, out_shape=jax.ShapeDtypeStruct((template_tot...]
    unnamed x22 -> x1, local copies, waits for them, and re-layouts: 6.35 us -> 1.32 us
    ppermute x1 -> x0, starting transfers between devices: 2.36 us -> none  [local(): prev = lax.ppermute(gated[-RADIX:], 'seg', pairs)]
    mul x1 -> x0, other arithmetic: 1.06 us -> none  [local(): gated = (strain * gate_mask.astype(F32)).reshape(-1, 128)]
    ppermute x1 -> x0, waiting for transfers between devices: 0.96 us -> none  [local(): prev = lax.ppermute(gated[-RADIX:], 'seg', pairs)]
  transfers between devices with their start and end apart: 2 -> 0, of which waited for: 2 -> 0; matrix products, arithmetic and copies ran while one was open for 1% -> 0% of each run, Pallas kernels for 2% -> 0%
where the time goes in v1:
time: 41.9 us; the launch traced here: 41.6 us
  Pallas kernels  38.7 us (92%)
  local copies, waits for them, and re-layouts  2.95 us (7%)
    pallas_call x1, Pallas kernels, fused(): pl.pallas_call(fused_kernel, out_shape=jax.ShapeDtypeStruct((template_tot...  38.7 us
    reshape x1, local copies, waits for them, and re-layouts, local(): template_bank.reshape(template_total, -1, RADIX)  1.63 us
    unnamed x1, local copies, waits for them, and re-layouts  1.32 us

profile of v1, /device:TPU:0, one launch (start us, length us, event | category | flops | bytes accessed | tf_op | source)
XLA Modules:
  0.0 41.6 jit_solution(4776940264458694218)
XLA Ops:
  0.0 1.6 %reshape.11.bank_ref = bf16[16,16,256]{2,1,0:T(8,128)(2,1)} reshape(bf16[16,2,2048]{2,1,0:T(2,128)(2,1)} %param.11) | data formatting | bytes 262144 | tf_op jit(solution)/shard_map/reshape | solution.py:335
  1.6 38.7 %matched_filter.1 = f32[16,256]{1,0:T(8,128)} custom-call(f32[512,128]{1,0:T(8,128)} %bitcast.2, s32[512,128]{1,0:T(8,128)} %bitcast.3, bf16[16,16,256]{2,1,0:T(8,128)(2,1)} %reshape.11.bank_ref, bf16[128,512]{1,0:T(8,128)(2,1)} %constant.12.clone.th_ref, bf16[128,512]{1,0:T(8,128)(2,1)} %constant.13.clone.tl_ref, f32[2,256,256]{2,1,0:T(8,128)} %constant.16.clone.w_ref, ...), custom_call_target="tpu_custom_call" | custom-call | tf_op jit(solution)/shard_map/matched_filter/pallas_call | solution.py:305
  40.3 1.3 %copy.11 = f32[16,256]{1,0:T(8,128)} copy(f32[16,256]{1,0:T(8,128)} %matched_filter.1) | data formatting | bytes 32768

commit v2 on v1

--- a/solution.py
+++ b/solution.py
@@ -21,6 +21,8 @@
 SEGS = 16
 GROUP = 2
 GROUPS = 8
+AHEAD = 4
+TABLES = 6
 
 
 def angles(rows, cols, period):
@@ -68,51 +70,50 @@
     return jnp.dot(left, right, preferred_element_type=F32)
 
 
-def inverse_kernel(h_ref, x_ref, t_ref, w_ref, u_ref, o_ref):
+def inverse_kernel(h_ref, x_ref, t_ref, w_ref, u_ref, o_ref, part_ref, scale_ref):
     index = pl.program_id(0)
-    peaks = template_peaks([(h_ref[0, 0], h_ref[0, 1])], x_ref, t_ref, w_ref, u_ref)[0]
+    bank_real, bank_imag = h_ref[0, 0].astype(F32), h_ref[0, 1].astype(F32)
+    first_product(bank_real, bank_imag, x_ref, t_ref, part_ref, scale_ref)
+    peaks = second_product(part_ref, scale_ref, w_ref, u_ref)
     row = lax.broadcasted_iota(jnp.int32, o_ref.shape, 0)
     o_ref[...] = jnp.where(row == index, peaks, o_ref[...])
 
 
-def template_peaks(banks, x_ref, t_ref, w_ref, u_ref):
-    wide = [(real.astype(F32), imag.astype(F32)) for real, imag in banks]
-    scales = [
-        1.0 / (BLOCK * jnp.sum(real * real + imag * imag) + EPSILON) for real, imag in wide
-    ]
-
-    def first(item):
-        bank_real, bank_imag = wide[item // 2]
-        real, imag = x_ref[item % 2, :HALF], x_ref[item % 2, HALF:]
+def first_product(bank_real, bank_imag, x_ref, t_ref, part_ref, scale_ref):
+    scale = 1.0 / (BLOCK * jnp.sum(bank_real * bank_real + bank_imag * bank_imag) + EPSILON)
+    scale_ref[...] = jnp.full(scale_ref.shape, scale, F32)
+    highs, lows = [], []
+    for block in range(2):
+        real, imag = x_ref[block, :HALF], x_ref[block, HALF:]
         high, low = split(
             jnp.concatenate(
                 [real * bank_real + imag * bank_imag, imag * bank_real - real * bank_imag], axis=0
             )
         )
-        return dot(t_ref[...], jnp.concatenate([high, high, low], axis=0))
-
-    def second(part):
-        real, imag = part[:RADIX], part[RADIX:]
-        cos, sin = w_ref[0], w_ref[1]
+        highs.append(high)
+        lows.append(low)
+    high, low = jnp.concatenate(highs, axis=1), jnp.concatenate(lows, axis=1)
+    part_ref[...] = dot(t_ref[...], jnp.concatenate([high, high, low], axis=0))
+
+
+def second_product(part_ref, scale_ref, w_ref, u_ref):
+    cos, sin = w_ref[0], w_ref[1]
+    rows = []
+    for block in range(2):
+        columns = slice(block * RADIX, (block + 1) * RADIX)
+        real, imag = part_ref[:RADIX, columns], part_ref[RADIX:, columns]
         high, low = split(
             jnp.concatenate([real * cos - imag * sin, real * sin + imag * cos], axis=1)
         )
-        return dot(jnp.concatenate([high, low, high], axis=1), u_ref[...])
-
-    def peak(series):
-        real, imag = series[:, :HALF], series[:, HALF:]
-        return jnp.max(real * real + imag * imag, axis=0, keepdims=True)
-
-    count = 2 * len(banks)
-    parts = [first(0)]
-    peaks = []
-    for item in range(count):
-        if item + 1 < count:
-            parts.append(first(item + 1))
-        peaks.append(peak(second(parts[item])))
-    return [
-        jnp.concatenate(peaks[2 * i : 2 * i + 2], axis=1) * scales[i] for i in range(len(banks))
+        rows.append(jnp.concatenate([high, low, high], axis=1))
+    series = dot(jnp.concatenate(rows, axis=0), u_ref[...])
+    real, imag = series[:, :HALF], series[:, HALF:]
+    power = real * real + imag * imag
+    peaks = [
+        jnp.max(power[block * RADIX : (block + 1) * RADIX], axis=0, keepdims=True)
+        for block in range(2)
     ]
+    return jnp.concatenate(peaks, axis=1) * scale_ref[...]
 
 
 def window_spectra(grids, th_ref, tl_ref, w_ref, u_ref, x_ref):
@@ -144,9 +145,12 @@
 
 
 def fused_kernel(
-    strain_ref, mask_ref, bank_ref, th_ref, tl_ref, w_ref, fu_ref, t_ref, u_ref, o_ref,
-    gated, prev, held, x_ref, prev_sem, own_send, pass_send, recv_sem,
+    strain_ref, mask_ref, bank_ref, *refs,
 ):
+    outside, refs = refs[:TABLES], refs[TABLES:]
+    o_ref, gated, prev, held, x_ref, part_a, part_b, scale_a, scale_b, *refs = refs
+    prev_sem, own_send, pass_send, recv_sem, table_sem, *tables = refs
+    th_ref, tl_ref, w_ref, fu_ref, t_ref, u_ref = tables
     me = lax.axis_index("seg")
     z_peers = [(me + 4 * step) % SEGS for step in range(1, 4)]
     y_peer = me + 2 - 4 * ((me // 2) % 2)
@@ -157,6 +161,11 @@
     for peer in (*z_peers, y_peer, sibling, (me + last) % SEGS):
         pl.semaphore_signal(barrier, inc=1, device_id={"seg": peer}, device_id_type=MESH)
 
+    table_copies = [
+        pltpu.make_async_copy(outside[i], tables[i], table_sem.at[i]) for i in range(TABLES)
+    ]
+    for copy in table_copies:
+        copy.start()
     gated[...] = strain_ref[...] * mask_ref[...].astype(F32)
     held[me] = bank_ref[...]
 
@@ -237,7 +246,7 @@
             copy.start()
         return carry
 
-    lax.fori_loop(0, GROUPS, start_own, 0)
+    lax.fori_loop(0, AHEAD, start_own, 0)
     o_ref[...] = jnp.zeros_like(o_ref)
 
     @pl.when(me == 0)
@@ -250,40 +259,52 @@
     def _():
         prev_copy().wait_recv()
 
+    for copy in table_copies:
+        copy.wait()
     pass_z(1)
     grids = [grid_of(prev, 0), grid_of(gated, 0), grid_of(gated, RADIX)]
     window_spectra(grids, th_ref, tl_ref, w_ref, fu_ref, x_ref)
     pass_y(0)
 
+    def first(template, part_ref, scale_ref):
+        rows = held[:, template].astype(F32)
+        half = rows.shape[1] // 2
+        bank_real = rows[:, :half].reshape(HALF, RADIX)
+        bank_imag = rows[:, half:].reshape(HALF, RADIX)
+        first_product(bank_real, bank_imag, x_ref, t_ref, part_ref, scale_ref)
+
+    def second(template, part_ref, scale_ref):
+        peaks = second_product(part_ref, scale_ref, w_ref, u_ref)
+        row = lax.broadcasted_iota(jnp.int32, o_ref.shape, 0)
+        o_ref[...] = jnp.where(row == template, peaks, o_ref[...])
+
+    def all_arrived(group):
+        for chunk in sibling_chunks():
+            arrived(group, chunk)
+
     def step(group, carry):
+        @pl.when(group + AHEAD < GROUPS)
+        def _():
+            start_own(group + AHEAD, 0)
+
         @pl.when(group + 2 < GROUPS)
         def _():
             pass_z(group + 2)
 
-        @pl.when(group + 1 < GROUPS)
-        def _():
-            pass_y(group + 1)
-
-        for chunk in sibling_chunks():
-            arrived(group, chunk)
-        banks = []
-        for item in range(GROUP):
-            rows = held[:, group * GROUP + item]
-            banks.append(
-                (rows[:, : rows.shape[1] // 2], rows[:, rows.shape[1] // 2 :])
-            )
-        banks = [
-            (real.astype(F32).reshape(HALF, RADIX), imag.astype(F32).reshape(HALF, RADIX))
-            for real, imag in banks
-        ]
-        row = lax.broadcasted_iota(jnp.int32, o_ref.shape, 0)
-        total = o_ref[...]
-        for item, peaks in enumerate(template_peaks(banks, x_ref, t_ref, w_ref, u_ref)):
-            total = jnp.where(row == group * GROUP + item, peaks, total)
-        o_ref[...] = total
+        pass_y(group + 1)
+        first(2 * group + 1, part_b, scale_b)
+        second(2 * group, part_a, scale_a)
+        all_arrived(group + 1)
+        first(2 * group + 2, part_a, scale_a)
+        second(2 * group + 1, part_b, scale_b)
         return carry
 
-    lax.fori_loop(0, GROUPS, step, 0)
+    all_arrived(0)
+    first(0, part_a, scale_a)
+    lax.fori_loop(0, GROUPS - 1, step, 0)
+    first(2 * GROUPS - 1, part_b, scale_b)
+    second(2 * GROUPS - 2, part_a, scale_a)
+    second(2 * GROUPS - 1, part_b, scale_b)
 
     def finish(group, carry):
         for copy in own_copies(group) + z_copies(group) + y_copies(group):
@@ -299,29 +320,34 @@
 
 def fused(strain, gate_mask, rows):
     template_total = rows.shape[0]
-    th, tl, fu = (jnp.asarray(t) for t in forward_tables())
-    t3, twist, u3 = (jnp.asarray(t) for t in inverse_tables())
+    th, tl, fu = forward_tables()
+    t3, twist, u3 = inverse_tables()
+    tables = [jnp.asarray(t) for t in (th, tl, twist, fu, t3, u3)]
     vmem = pl.BlockSpec(memory_space=pltpu.VMEM)
     return pl.pallas_call(
         fused_kernel,
         out_shape=jax.ShapeDtypeStruct((template_total, RADIX), F32),
-        in_specs=[vmem] * 9,
+        in_specs=[vmem] * 3 + [pl.BlockSpec(memory_space=pl.ANY)] * TABLES,
         out_specs=vmem,
         scratch_shapes=[
             pltpu.VMEM((2 * RADIX, 128), F32),
             pltpu.VMEM((RADIX, 128), F32),
             pltpu.VMEM((SEGS, *rows.shape), BF16),
             pltpu.VMEM((2, RADIX, RADIX), F32),
+            *[pltpu.VMEM((2 * RADIX, 2 * RADIX), F32)] * 2,
+            *[pltpu.VMEM((1, RADIX), F32)] * 2,
             pltpu.SemaphoreType.DMA((2,)),
             pltpu.SemaphoreType.DMA((GROUPS, 5)),
             pltpu.SemaphoreType.DMA((GROUPS, 10)),
             pltpu.SemaphoreType.DMA((GROUPS, SEGS)),
+            pltpu.SemaphoreType.DMA((TABLES,)),
+            *(pltpu.VMEM(table.shape, table.dtype) for table in tables),
         ],
         compiler_params=pltpu.CompilerParams(
             vmem_limit_bytes=VMEM_LIMIT, collective_id=0, has_side_effects=True
         ),
         name="matched_filter",
-    )(strain.reshape(-1, 128), gate_mask.reshape(-1, 128), rows, th, tl, twist, fu, t3, u3)
+    )(strain.reshape(-1, 128), gate_mask.reshape(-1, 128), rows, *tables)
 
 
 def whole(shape):
@@ -358,6 +384,7 @@
             *(whole(t.shape) for t in tables),
         ],
         out_specs=whole((template_total, RADIX)),
+        scratch_shapes=[pltpu.VMEM((2 * RADIX, 2 * RADIX), F32), pltpu.VMEM((1, RADIX), F32)],
         compiler_params=params,
         name="series_peaks",
     )(bank, spectra, *tables)

time: 41.9 us -> 41.8 us (level)
  no operation moved by 1% of the time
where the time goes in v2:
time: 41.8 us; the launch traced here: 41.5 us
  Pallas kernels  38.6 us (92%)
  local copies, waits for them, and re-layouts  2.95 us (7%)
    pallas_call x1, Pallas kernels, fused(): pl.pallas_call(fused_kernel, out_shape=jax.ShapeDtypeStruct((template_tot...  38.6 us
    reshape x1, local copies, waits for them, and re-layouts, local(): template_bank.reshape(template_total, -1, RADIX)  1.63 us
    unnamed x1, local copies, waits for them, and re-layouts  1.32 us

profile of v2, /device:TPU:0, one launch (start us, length us, event | category | flops | bytes accessed | tf_op | source)
XLA Modules:
  0.0 41.5 jit_solution(16047324826279271454)
XLA Ops:
  0.0 1.6 %reshape.11.bank_ref = bf16[16,16,256]{2,1,0:T(8,128)(2,1)} reshape(bf16[16,2,2048]{2,1,0:T(2,128)(2,1)} %param.11) | data formatting | bytes 262144 | tf_op jit(solution)/shard_map/reshape | solution.py:361
  1.6 38.6 %matched_filter.1 = f32[16,256]{1,0:T(8,128)} custom-call(f32[512,128]{1,0:T(8,128)} %bitcast.2, s32[512,128]{1,0:T(8,128)} %bitcast.3, bf16[16,16,256]{2,1,0:T(8,128)(2,1)} %reshape.11.bank_ref, bf16[128,512]{1,0:T(8,128)(2,1)} %constant.12.clone.refs_0_, bf16[128,512]{1,0:T(8,128)(2,1)} %constant.13.clone.refs_1_, f32[2,256,256]{2,1,0:T(8,128)} %constant.14.clone.refs_2_, ...), custom_call_target="tpu_custom_call" | custom-call | tf_op jit(solution)/shard_map/matched_filter/pallas_call | solution.py:327
  40.2 1.3 %copy.11 = f32[16,256]{1,0:T(8,128)} copy(f32[16,256]{1,0:T(8,128)} %matched_filter.1) | data formatting | bytes 32768

commit v3 on v2

--- a/solution.py
+++ b/solution.py
@@ -16,13 +16,18 @@
 EPSILON = 1e-06
 BF16 = jnp.bfloat16
 F32 = jnp.float32
+F8 = jnp.float8_e4m3fn
+LIFT = 4096.0
+NARROW = 16.0
+SHRINK = 128.0
+TOP = 16.0
 MESH = pl.DeviceIdType.MESH
 VMEM_LIMIT = 56 * 1024 * 1024
 SEGS = 16
 GROUP = 2
 GROUPS = 8
 AHEAD = 4
-TABLES = 6
+TABLES = 8
 
 
 def angles(rows, cols, period):
@@ -49,16 +54,20 @@
 @functools.cache
 def inverse_tables():
     cos, sin = angles(RADIX, HALF, RADIX)
-    first = two_parts(np.block([[cos, -sin], [sin, cos]]))
+    high, low = two_parts(np.block([[cos, -sin], [sin, cos]]))
+    first = (high.astype(np.float64) * LIFT).astype(ml_dtypes.bfloat16)
+    first_rest = np.concatenate([small(high.astype(np.float64) * NARROW), small(low.astype(np.float64) * LIFT)], axis=1)
     cos, sin = angles(RADIX, RADIX, RADIX * RADIX)
     twist = np.stack([cos, sin]).astype(np.float32)
     cos, sin = angles(RADIX, HALF, RADIX)
-    second = two_parts(np.block([[cos, sin], [-sin, cos]]))
-    return (
-        np.concatenate([first[0], first[1], first[0]], axis=1),
-        twist,
-        np.concatenate([second[0], second[0], second[1]], axis=0),
-    )
+    high, low = two_parts(np.block([[cos, sin], [-sin, cos]]))
+    second = (high.astype(np.float64) * LIFT).astype(ml_dtypes.bfloat16)
+    second_rest = np.concatenate([small(high.astype(np.float64) * NARROW), small(low.astype(np.float64) * LIFT)], axis=0)
+    return first, first_rest, twist, second, second_rest
+
+
+def small(table):
+    return table.astype(np.float64).astype(ml_dtypes.float8_e4m3fn)
 
 
 def split(value):
@@ -66,57 +75,69 @@
     return high, (value - high.astype(F32)).astype(BF16)
 
 
+def split_small(value):
+    high = value.astype(BF16)
+    rest = ((value - high.astype(F32)) * (LIFT / NARROW)).astype(F8)
+    return high, rest, value.astype(F8)
+
+
 def dot(left, right):
     return jnp.dot(left, right, preferred_element_type=F32)
 
 
-def inverse_kernel(h_ref, x_ref, t_ref, w_ref, u_ref, o_ref, part_ref, scale_ref):
+def inverse_kernel(h_ref, x_ref, gain_ref, t_ref, tr_ref, w_ref, u_ref, ur_ref, o_ref, part_ref, scale_ref):
     index = pl.program_id(0)
     bank_real, bank_imag = h_ref[0, 0].astype(F32), h_ref[0, 1].astype(F32)
-    first_product(bank_real, bank_imag, x_ref, t_ref, part_ref, scale_ref)
-    peaks = second_product(part_ref, scale_ref, w_ref, u_ref)
+    first_product(bank_real, bank_imag, x_ref, t_ref, tr_ref, part_ref, scale_ref)
+    peaks = second_product(part_ref, scale_ref, gain_ref, w_ref, u_ref, ur_ref)
     row = lax.broadcasted_iota(jnp.int32, o_ref.shape, 0)
     o_ref[...] = jnp.where(row == index, peaks, o_ref[...])
 
 
-def first_product(bank_real, bank_imag, x_ref, t_ref, part_ref, scale_ref):
+def first_product(bank_real, bank_imag, x_ref, t_ref, tr_ref, part_ref, scale_ref):
     scale = 1.0 / (BLOCK * jnp.sum(bank_real * bank_real + bank_imag * bank_imag) + EPSILON)
     scale_ref[...] = jnp.full(scale_ref.shape, scale, F32)
-    highs, lows = [], []
+    pieces = []
     for block in range(2):
         real, imag = x_ref[block, :HALF], x_ref[block, HALF:]
-        high, low = split(
-            jnp.concatenate(
-                [real * bank_real + imag * bank_imag, imag * bank_real - real * bank_imag], axis=0
+        pieces.append(
+            split_small(
+                jnp.concatenate(
+                    [real * bank_real + imag * bank_imag, imag * bank_real - real * bank_imag],
+                    axis=0,
+                )
             )
         )
-        highs.append(high)
-        lows.append(low)
-    high, low = jnp.concatenate(highs, axis=1), jnp.concatenate(lows, axis=1)
-    part_ref[...] = dot(t_ref[...], jnp.concatenate([high, high, low], axis=0))
-
-
-def second_product(part_ref, scale_ref, w_ref, u_ref):
-    cos, sin = w_ref[0], w_ref[1]
-    rows = []
+    high, rest, value = (jnp.concatenate(pair, axis=1) for pair in zip(*pieces))
+    part_ref[...] = dot(t_ref[...], high) + dot(
+        tr_ref[...], jnp.concatenate([rest, value], axis=0)
+    )
+
+
+def second_product(part_ref, scale_ref, gain_ref, w_ref, u_ref, ur_ref):
+    cos, sin = w_ref[0] * (1.0 / (LIFT * SHRINK)), w_ref[1] * (1.0 / (LIFT * SHRINK))
+    pieces = []
     for block in range(2):
         columns = slice(block * RADIX, (block + 1) * RADIX)
         real, imag = part_ref[:RADIX, columns], part_ref[RADIX:, columns]
-        high, low = split(
+        high, rest, value = split_small(
             jnp.concatenate([real * cos - imag * sin, real * sin + imag * cos], axis=1)
         )
-        rows.append(jnp.concatenate([high, low, high], axis=1))
-    series = dot(jnp.concatenate(rows, axis=0), u_ref[...])
+        pieces.append((high, jnp.concatenate([rest, value], axis=1)))
+    high, small_parts = (jnp.concatenate(pair, axis=0) for pair in zip(*pieces))
+    series = dot(high, u_ref[...]) + dot(small_parts, ur_ref[...])
     real, imag = series[:, :HALF], series[:, HALF:]
     power = real * real + imag * imag
     peaks = [
         jnp.max(power[block * RADIX : (block + 1) * RADIX], axis=0, keepdims=True)
         for block in range(2)
     ]
-    return jnp.concatenate(peaks, axis=1) * scale_ref[...]
-
-
-def window_spectra(grids, th_ref, tl_ref, w_ref, u_ref, x_ref):
+    gain = gain_ref[...]
+    both = jnp.concatenate(peaks, axis=1) * ((SHRINK / LIFT) ** 2 * scale_ref[...])
+    return both * gain * gain
+
+
+def window_spectra(grids, th_ref, tl_ref, w_ref, u_ref, x_ref, gain_ref):
     def first_stage(grid):
         high, low = split(grid)
         return dot(high, th_ref[...]) + dot(low, th_ref[...]) + dot(high, tl_ref[...])
@@ -131,7 +152,10 @@
         high, low = split(
             jnp.concatenate([real * cos + imag * sin, imag * cos - real * sin], axis=0)
         )
-        x_ref[block] = dot(u_ref[...], jnp.concatenate([high, high, low], axis=0))
+        spectra = dot(u_ref[...], jnp.concatenate([high, high, low], axis=0))
+        gain = jnp.maximum(jnp.max(jnp.abs(spectra)), 1e-30) * (1.0 / TOP)
+        gain_ref[:, block * HALF : (block + 1) * HALF] = jnp.full((1, HALF), gain, F32)
+        x_ref[block] = spectra * (1.0 / gain)
 
 
 def grid_of(ref, start):
@@ -139,18 +163,18 @@
     return jnp.concatenate([half.T for half in halves], axis=0)
 
 
-def forward_kernel(g_ref, prev_ref, th_ref, tl_ref, w_ref, u_ref, x_ref):
+def forward_kernel(g_ref, prev_ref, th_ref, tl_ref, w_ref, u_ref, x_ref, gain_ref):
     grids = [grid_of(prev_ref, 0), grid_of(g_ref, 0), grid_of(g_ref, RADIX)]
-    window_spectra(grids, th_ref, tl_ref, w_ref, u_ref, x_ref)
+    window_spectra(grids, th_ref, tl_ref, w_ref, u_ref, x_ref, gain_ref)
 
 
 def fused_kernel(
     strain_ref, mask_ref, bank_ref, *refs,
 ):
     outside, refs = refs[:TABLES], refs[TABLES:]
-    o_ref, gated, prev, held, x_ref, part_a, part_b, scale_a, scale_b, *refs = refs
+    o_ref, gated, prev, held, x_ref, gain_ref, part_a, part_b, scale_a, scale_b, *refs = refs
     prev_sem, own_send, pass_send, recv_sem, table_sem, *tables = refs
-    th_ref, tl_ref, w_ref, fu_ref, t_ref, u_ref = tables
+    th_ref, tl_ref, fu_ref, t_ref, tr_ref, w_ref, u_ref, ur_ref = tables
     me = lax.axis_index("seg")
     z_peers = [(me + 4 * step) % SEGS for step in range(1, 4)]
     y_peer = me + 2 - 4 * ((me // 2) % 2)
@@ -263,7 +287,7 @@
         copy.wait()
     pass_z(1)
     grids = [grid_of(prev, 0), grid_of(gated, 0), grid_of(gated, RADIX)]
-    window_spectra(grids, th_ref, tl_ref, w_ref, fu_ref, x_ref)
+    window_spectra(grids, th_ref, tl_ref, w_ref, fu_ref, x_ref, gain_ref)
     pass_y(0)
 
     def first(template, part_ref, scale_ref):
@@ -271,10 +295,10 @@
         half = rows.shape[1] // 2
         bank_real = rows[:, :half].reshape(HALF, RADIX)
         bank_imag = rows[:, half:].reshape(HALF, RADIX)
-        first_product(bank_real, bank_imag, x_ref, t_ref, part_ref, scale_ref)
+        first_product(bank_real, bank_imag, x_ref, t_ref, tr_ref, part_ref, scale_ref)
 
     def second(template, part_ref, scale_ref):
-        peaks = second_product(part_ref, scale_ref, w_ref, u_ref)
+        peaks = second_product(part_ref, scale_ref, gain_ref, w_ref, u_ref, ur_ref)
         row = lax.broadcasted_iota(jnp.int32, o_ref.shape, 0)
         o_ref[...] = jnp.where(row == template, peaks, o_ref[...])
 
@@ -320,9 +344,7 @@
 
 def fused(strain, gate_mask, rows):
     template_total = rows.shape[0]
-    th, tl, fu = forward_tables()
-    t3, twist, u3 = inverse_tables()
-    tables = [jnp.asarray(t) for t in (th, tl, twist, fu, t3, u3)]
+    tables = [jnp.asarray(t) for t in (*forward_tables(), *inverse_tables())]
     vmem = pl.BlockSpec(memory_space=pltpu.VMEM)
     return pl.pallas_call(
         fused_kernel,
@@ -334,6 +356,7 @@
             pltpu.VMEM((RADIX, 128), F32),
             pltpu.VMEM((SEGS, *rows.shape), BF16),
             pltpu.VMEM((2, RADIX, RADIX), F32),
+            pltpu.VMEM((1, RADIX), F32),
             *[pltpu.VMEM((2 * RADIX, 2 * RADIX), F32)] * 2,
             *[pltpu.VMEM((1, RADIX), F32)] * 2,
             pltpu.SemaphoreType.DMA((2,)),
@@ -365,15 +388,17 @@
     rows = template_bank.reshape(template_total, 2, -1, RADIX)
     bank = lax.all_gather(rows, "seg", axis=2, tiled=True)
     th, tl, fu = (jnp.asarray(t) for t in forward_tables())
-    t3, twist, u3 = (jnp.asarray(t) for t in inverse_tables())
+    tables = [jnp.asarray(t) for t in inverse_tables()]
     params = pltpu.CompilerParams(vmem_limit_bytes=VMEM_LIMIT)
-    spectra = pl.pallas_call(
+    spectra, gain = pl.pallas_call(
         forward_kernel,
-        out_shape=jax.ShapeDtypeStruct((2, RADIX, RADIX), F32),
+        out_shape=(
+            jax.ShapeDtypeStruct((2, RADIX, RADIX), F32),
+            jax.ShapeDtypeStruct((1, RADIX), F32),
+        ),
         compiler_params=params,
         name="window_spectra",
-    )(gated, prev, th, tl, twist, fu)
-    tables = (t3, twist, u3)
+    )(gated, prev, th, tl, tables[2], fu)
     return pl.pallas_call(
         inverse_kernel,
         out_shape=jax.ShapeDtypeStruct((template_total, RADIX), F32),
@@ -381,13 +406,14 @@
         in_specs=[
             pl.BlockSpec((1, 2, HALF, RADIX), lambda k: (k, 0, 0, 0)),
             whole((2, RADIX, RADIX)),
+            whole((1, RADIX)),
             *(whole(t.shape) for t in tables),
         ],
         out_specs=whole((template_total, RADIX)),
         scratch_shapes=[pltpu.VMEM((2 * RADIX, 2 * RADIX), F32), pltpu.VMEM((1, RADIX), F32)],
         compiler_params=params,
         name="series_peaks",
-    )(bank, spectra, *tables)
+    )(bank, spectra, gain, *tables)
 
 
 def solution(mesh):

time: 41.8 us -> 41.9 us (level)
  no operation moved by 1% of the time
where the time goes in v3:
time: 41.9 us; the launch traced here: 41.6 us
  Pallas kernels  38.7 us (92%)
  local copies, waits for them, and re-layouts  2.95 us (7%)
    pallas_call x1, Pallas kernels, fused(): pl.pallas_call(fused_kernel, out_shape=jax.ShapeDtypeStruct((template_tot...  38.7 us
    reshape x1, local copies, waits for them, and re-layouts, local(): template_bank.reshape(template_total, -1, RADIX)  1.63 us
    unnamed x1, local copies, waits for them, and re-layouts  1.32 us

profile of v3, /device:TPU:0, one launch (start us, length us, event | category | flops | bytes accessed | tf_op | source)
XLA Modules:
  0.0 41.6 jit_solution(12861001739218506160)
XLA Ops:
  0.0 1.6 %reshape.11.bank_ref = bf16[16,16,256]{2,1,0:T(8,128)(2,1)} reshape(bf16[16,2,2048]{2,1,0:T(2,128)(2,1)} %param.13) | data formatting | bytes 262144 | tf_op jit(solution)/shard_map/reshape | solution.py:384
  1.6 38.7 %matched_filter.1 = f32[16,256]{1,0:T(8,128)} custom-call(f32[512,128]{1,0:T(8,128)} %bitcast.2, s32[512,128]{1,0:T(8,128)} %bitcast.3, bf16[16,16,256]{2,1,0:T(8,128)(2,1)} %reshape.11.bank_ref, bf16[128,512]{1,0:T(8,128)(2,1)} %constant.16.clone.refs_0_, bf16[128,512]{1,0:T(8,128)(2,1)} %constant.17.clone.refs_1_, ...), custom_call_target="tpu_custom_call" | custom-call | tf_op jit(solution)/shard_map/matched_filter/pallas_call | solution.py:349
  40.3 1.3 %copy.13 = f32[16,256]{1,0:T(8,128)} copy(f32[16,256]{1,0:T(8,128)} %matched_filter.1) | data formatting | bytes 32768

commit v4 on v3

v4 whole, which is shorter than its diff:
```python
import functools
import math

import jax
import jax.numpy as jnp
import ml_dtypes
import numpy as np
from jax import lax
from jax.experimental import pallas as pl
from jax.experimental.pallas import tpu as pltpu
from jax.sharding import PartitionSpec as P

RADIX = 256
HALF = RADIX // 2
BLOCK = 32768
EPSILON = 1e-06
BF16 = jnp.bfloat16
F32 = jnp.float32
F8 = jnp.float8_e4m3fn
LIFT = 4096.0
NARROW = 16.0
SHRINK = 128.0
TOP = 16.0
MESH = pl.DeviceIdType.MESH
VMEM_LIMIT = 56 * 1024 * 1024
SEGS = 16
GROUP = 2
GROUPS = 4
CHIPS = 8
TABLES = 8


def angles(rows, cols, period):
    phase = np.outer(np.arange(rows), np.arange(cols)) % period
    turn = phase * (2.0 * math.pi / period)
    return np.cos(turn), np.sin(turn)


def two_parts(table):
    high = table.astype(ml_dtypes.bfloat16)
    low = (table - high.astype(np.float64)).astype(ml_dtypes.bfloat16)
    return high, low


@functools.cache
def forward_tables():
    cos, sin = angles(HALF, RADIX, RADIX)
    high, low = two_parts(np.concatenate([cos, -sin], axis=1))
    cos, sin = angles(HALF, RADIX, RADIX)
    second = two_parts(np.block([[cos, sin], [-sin, cos]]))
    return high, low, np.concatenate([second[0], second[1], second[0]], axis=1)


@functools.cache
def inverse_tables():
    cos, sin = angles(RADIX, HALF, RADIX)
    high, low = two_parts(np.block([[cos, -sin], [sin, cos]]))
    first = (high.astype(np.float64) * LIFT).astype(ml_dtypes.bfloat16)
    first_rest = np.concatenate([small(high.astype(np.float64) * NARROW), small(low.astype(np.float64) * LIFT)], axis=1)
    cos, sin = angles(RADIX, RADIX, RADIX * RADIX)
    twist = np.stack([cos, sin]).astype(np.float32)
    cos, sin = angles(RADIX, HALF, RADIX)
    high, low = two_parts(np.block([[cos, sin], [-sin, cos]]))
    second = (high.astype(np.float64) * LIFT).astype(ml_dtypes.bfloat16)
    second_rest = np.concatenate([small(high.astype(np.float64) * NARROW), small(low.astype(np.float64) * LIFT)], axis=0)
    return first, first_rest, twist, second, second_rest


def small(table):
    return table.astype(np.float64).astype(ml_dtypes.float8_e4m3fn)


def split(value):
    high = value.astype(BF16)
    return high, (value - high.astype(F32)).astype(BF16)


def split_small(value):
    high = value.astype(BF16)
    rest = ((value - high.astype(F32)) * (LIFT / NARROW)).astype(F8)
    return high, rest, value.astype(F8)


def dot(left, right):
    return jnp.dot(left, right, preferred_element_type=F32)


def inverse_kernel(h_ref, x_ref, gain_ref, t_ref, tr_ref, w_ref, u_ref, ur_ref, o_ref, part_ref, scale_ref):
    index = pl.program_id(0)
    bank_real, bank_imag = h_ref[0, 0].astype(F32), h_ref[0, 1].astype(F32)
    windows = [(x_ref[block, :HALF], x_ref[block, HALF:]) for block in range(2)]
    first_product(bank_real, bank_imag, windows, t_ref, tr_ref, part_ref, scale_ref)
    peaks = second_product(part_ref, scale_ref, gain_ref[:1], w_ref, u_ref, ur_ref)
    row = lax.broadcasted_iota(jnp.int32, o_ref.shape, 0)
    o_ref[...] = jnp.where(row == index, peaks, o_ref[...])


def first_product(bank_real, bank_imag, windows, t_ref, tr_ref, part_ref, scale_ref):
    scale = 1.0 / (BLOCK * jnp.sum(bank_real * bank_real + bank_imag * bank_imag) + EPSILON)
    scale_ref[...] = jnp.full(scale_ref.shape, scale, F32)
    pieces = []
    for real, imag in windows:
        pieces.append(
            split_small(
                jnp.concatenate(
                    [real * bank_real + imag * bank_imag, imag * bank_real - real * bank_imag],
                    axis=0,
                )
            )
        )
    high, rest, value = (jnp.concatenate(pair, axis=1) for pair in zip(*pieces))
    part_ref[...] = dot(t_ref[...], high) + dot(
        tr_ref[...], jnp.concatenate([rest, value], axis=0)
    )


def second_product(part_ref, scale_ref, gain, w_ref, u_ref, ur_ref):
    cos, sin = w_ref[0] * (1.0 / (LIFT * SHRINK)), w_ref[1] * (1.0 / (LIFT * SHRINK))
    pieces = []
    for block in range(2):
        columns = slice(block * RADIX, (block + 1) * RADIX)
        real, imag = part_ref[:RADIX, columns], part_ref[RADIX:, columns]
        high, rest, value = split_small(
            jnp.concatenate([real * cos - imag * sin, real * sin + imag * cos], axis=1)
        )
        pieces.append((high, jnp.concatenate([rest, value], axis=1)))
    high, small_parts = (jnp.concatenate(pair, axis=0) for pair in zip(*pieces))
    series = dot(high, u_ref[...]) + dot(small_parts, ur_ref[...])
    real, imag = series[:, :HALF], series[:, HALF:]
    power = real * real + imag * imag
    peaks = [
        jnp.max(power[block * RADIX : (block + 1) * RADIX], axis=0, keepdims=True)
        for block in range(2)
    ]
    both = jnp.concatenate(peaks, axis=1) * ((SHRINK / LIFT) ** 2 * scale_ref[...])
    return both * gain * gain


def window_spectra(grids, th_ref, tl_ref, w_ref, u_ref):
    def first_stage(grid):
        high, low = split(grid)
        return dot(high, th_ref[...]) + dot(low, th_ref[...]) + dot(high, tl_ref[...])

    parity = lax.broadcasted_iota(jnp.int32, (RADIX, 2 * RADIX), 1) % 2
    sign = (1 - 2 * parity).astype(F32)
    blocks = [first_stage(grid) for grid in grids]
    windows, gains = [], []
    for block in range(2):
        both = blocks[block + 1] + sign * blocks[block]
        real, imag = both[:, :RADIX], both[:, RADIX:]
        cos, sin = w_ref[0], w_ref[1]
        high, low = split(
            jnp.concatenate([real * cos + imag * sin, imag * cos - real * sin], axis=0)
        )
        spectra = dot(u_ref[...], jnp.concatenate([high, high, low], axis=0))
        gain = jnp.maximum(jnp.max(jnp.abs(spectra)), 1e-30) * (1.0 / TOP)
        gains.append(jnp.full((8, HALF), gain, F32))
        windows.append(spectra * (1.0 / gain))
    return windows, jnp.concatenate(gains, axis=1)


def grid_of(ref, start):
    halves = [ref[pl.ds(start + half, HALF, stride=2), :] for half in range(2)]
    return jnp.concatenate([half.T for half in halves], axis=0)


def forward_kernel(g_ref, prev_ref, th_ref, tl_ref, w_ref, u_ref, x_ref, gain_ref):
    grids = [grid_of(prev_ref, 0), grid_of(g_ref, 0), grid_of(g_ref, RADIX)]
    windows, gain_ref[...] = window_spectra(grids, th_ref, tl_ref, w_ref, u_ref)
    x_ref[0], x_ref[1] = windows


def fused_kernel(strain_ref, mask_ref, bank_ref, *refs):
    outside, refs = refs[:TABLES], refs[TABLES:]
    o_ref, gated, prev, held, x_ref, peak_ref, got_ref, part_a, part_b, scale_a, scale_b, *refs = refs
    prev_sem, swap_send, swap_recv, own_send, pass_send, recv_sem, side_sem, table_sem, *tables = refs
    th_ref, tl_ref, fu_ref, t_ref, tr_ref, w_ref, u_ref, ur_ref = tables
    me = lax.axis_index("seg")
    core, chip = me % 2, me // 2
    z_peers = [(me + 4 * step) % SEGS for step in range(1, 4)]
    z_chips = [(chip + 2 * step) % CHIPS for step in range(1, 4)]
    y_peer = me + 2 - 4 * (chip % 2)
    y_chips = [(chip + 1 - 2 * (chip % 2) + 2 * step) % CHIPS for step in range(4)]
    sibling = me + 1 - 2 * core
    last = SEGS - 1
    share = bank_ref.shape[0] // 2

    barrier = pltpu.get_barrier_semaphore()
    for peer in (*z_peers, y_peer, sibling, (me + last) % SEGS):
        pl.semaphore_signal(barrier, inc=1, device_id={"seg": peer}, device_id_type=MESH)

    table_copies = [
        pltpu.make_async_copy(outside[i], tables[i], table_sem.at[i]) for i in range(TABLES)
    ]
    for copy in table_copies:
        copy.start()
    gated[...] = strain_ref[...] * mask_ref[...].astype(F32)
    held[chip, :, core] = bank_ref[pl.ds(core * share, share)]

    pl.semaphore_wait(barrier, 6)

    def remote(source, target, send_sem, got_sem, peer):
        return pltpu.make_async_remote_copy(
            src_ref=source,
            dst_ref=target,
            send_sem=send_sem,
            recv_sem=got_sem,
            device_id={"seg": peer},
            device_id_type=MESH,
        )

    def prev_copy():
        tail = gated.at[pl.ds(RADIX, RADIX)]
        return remote(tail, prev, prev_sem.at[0], prev_sem.at[1], me + 1)

    def swap_copy(group):
        return remote(
            bank_ref.at[pl.ds((1 - core) * share + group * GROUP, GROUP)],
            held.at[chip, pl.ds(group * GROUP, GROUP), core],
            swap_send.at[group],
            swap_recv.at[group],
            sibling,
        )

    def chunk_copy(group, source, send_sem, peer):
        piece = held.at[source, pl.ds(group * GROUP, GROUP)]
        return remote(piece, piece, send_sem, recv_sem.at[group, source], peer)

    def own_copies(group):
        return [
            chunk_copy(group, chip, own_send.at[group, i], peer)
            for i, peer in enumerate((*z_peers, y_peer))
        ]

    def z_copies(group):
        return [
            chunk_copy(group, source, pass_send.at[group, i], y_peer)
            for i, source in enumerate(z_chips)
        ]

    def x_copy():
        return remote(x_ref.at[core], x_ref.at[core], side_sem.at[0], side_sem.at[1], sibling)

    def peak_copy():
        return remote(peak_ref.at[1 - core], got_ref, side_sem.at[2], side_sem.at[3], sibling)

    def own(group):
        swap_copy(group).wait_recv()
        for copy in own_copies(group):
            copy.start()

    def pass_z(group):
        for copy in z_copies(group):
            copy.wait_recv()
            copy.start()

    def all_arrived(group):
        for source in y_chips:
            chunk_copy(group, source, own_send.at[group, 0], y_peer).wait_recv()

    for group in range(GROUPS):
        swap_copy(group).start()

    @pl.when(me < last)
    def _():
        prev_copy().start()

    own(0)
    own(1)
    peak_ref[...] = jnp.zeros_like(peak_ref)

    @pl.when(me == 0)
    def _():
        prev[...] = jnp.zeros_like(prev)

    pass_z(0)

    @pl.when(me > 0)
    def _():
        prev_copy().wait_recv()

    own(2)
    for copy in table_copies:
        copy.wait()
    grids = [grid_of(prev, 0), grid_of(gated, 0), grid_of(gated, RADIX)]
    windows, gains = window_spectra(grids, th_ref, tl_ref, w_ref, fu_ref)
    x_ref[core] = jnp.concatenate([*windows, gains], axis=0)
    x_copy().start()
    pass_z(1)
    own(3)

    def first(template, side, part_ref, scale_ref):
        rows = held[:, template].astype(F32).reshape(SEGS, -1, RADIX)
        half = rows.shape[1] // 2
        bank_real = rows[:, :half].reshape(HALF, RADIX)
        bank_imag = rows[:, half:].reshape(HALF, RADIX)
        windows = [
            (x_ref[side, at : at + HALF], x_ref[side, at + HALF : at + RADIX]) for at in (0, RADIX)
        ]
        first_product(bank_real, bank_imag, windows, t_ref, tr_ref, part_ref, scale_ref)

    def second(template, side, part_ref, scale_ref):
        gain = x_ref[side, 2 * RADIX : 2 * RADIX + 1]
        peaks = second_product(part_ref, scale_ref, gain, w_ref, u_ref, ur_ref)
        row = lax.broadcasted_iota(jnp.int32, got_ref.shape, 0)
        peak_ref[side] = jnp.where(row == template, peaks, peak_ref[side])

    def pair(template, more):
        first(template, 1, part_b, scale_b)
        second(template, 0, part_a, scale_a)
        if more:
            first(template + 1, 0, part_a, scale_a)
        second(template, 1, part_b, scale_b)

    def step(group, carry):
        @pl.when(group + 2 < GROUPS)
        def _():
            pass_z(group + 2)

        pair(2 * group, True)
        all_arrived(group + 1)
        pair(2 * group + 1, True)
        return carry

    all_arrived(0)
    x_copy().wait_recv()
    first(0, 0, part_a, scale_a)
    lax.fori_loop(0, GROUPS - 1, step, 0)
    pair(2 * GROUPS - 2, True)
    pair(2 * GROUPS - 1, False)

    peak_copy().start()
    for group in range(GROUPS):
        for copy in (swap_copy(group), *own_copies(group), *z_copies(group)):
            copy.wait_send()
    x_copy().wait_send()

    @pl.when(me < last)
    def _():
        prev_copy().wait_send()

    peak_copy().wait()
    mine, other = peak_ref[core], got_ref[...]
    o_ref[:share] = jnp.where(core == 0, mine, other)
    o_ref[share:] = jnp.where(core == 0, other, mine)


def fused(strain, gate_mask, rows):
    template_total = rows.shape[0]
    tables = [jnp.asarray(t) for t in (*forward_tables(), *inverse_tables())]
    vmem = pl.BlockSpec(memory_space=pltpu.VMEM)
    return pl.pallas_call(
        fused_kernel,
        out_shape=jax.ShapeDtypeStruct((template_total, RADIX), F32),
        in_specs=[vmem] * 3 + [pl.BlockSpec(memory_space=pl.ANY)] * TABLES,
        out_specs=vmem,
        scratch_shapes=[
            pltpu.VMEM((2 * RADIX, 128), F32),
            pltpu.VMEM((RADIX, 128), F32),
            pltpu.VMEM((CHIPS, template_total // 2, 2, *rows.shape[1:]), BF16),
            pltpu.VMEM((2, 2 * RADIX + 8, RADIX), F32),
            pltpu.VMEM((2, template_total // 2, RADIX), F32),
            pltpu.VMEM((template_total // 2, RADIX), F32),
            *[pltpu.VMEM((2 * RADIX, 2 * RADIX), F32)] * 2,
            *[pltpu.VMEM((1, RADIX), F32)] * 2,
            pltpu.SemaphoreType.DMA((2,)),
            pltpu.SemaphoreType.DMA((GROUPS,)),
            pltpu.SemaphoreType.DMA((GROUPS,)),
            pltpu.SemaphoreType.DMA((GROUPS, 4)),
            pltpu.SemaphoreType.DMA((GROUPS, 3)),
            pltpu.SemaphoreType.DMA((GROUPS, CHIPS)),
            pltpu.SemaphoreType.DMA((4,)),
            pltpu.SemaphoreType.DMA((TABLES,)),
            *(pltpu.VMEM(table.shape, table.dtype) for table in tables),
        ],
        compiler_params=pltpu.CompilerParams(
            vmem_limit_bytes=VMEM_LIMIT, collective_id=0, has_side_effects=True
        ),
        name="matched_filter",
    )(strain.reshape(-1, 128), gate_mask.reshape(-1, 128), rows, *tables)


def whole(shape):
    return pl.BlockSpec(shape, lambda *_: (0,) * len(shape))


def local(strain, gate_mask, template_bank):
    template_total = template_bank.shape[0]
    count = lax.axis_size("seg")
    if count == SEGS and template_total == 2 * GROUP * GROUPS:
        return fused(strain, gate_mask, template_bank.reshape(template_total, -1, RADIX))
    gated = (strain * gate_mask.astype(F32)).reshape(-1, 128)
    pairs = [(i, i + 1) for i in range(count - 1)]
    prev = lax.ppermute(gated[-RADIX:], "seg", pairs)
    rows = template_bank.reshape(template_total, 2, -1, RADIX)
    bank = lax.all_gather(rows, "seg", axis=2, tiled=True)
    th, tl, fu = (jnp.asarray(t) for t in forward_tables())
    tables = [jnp.asarray(t) for t in inverse_tables()]
    params = pltpu.CompilerParams(vmem_limit_bytes=VMEM_LIMIT)
    spectra, gain = pl.pallas_call(
        forward_kernel,
        out_shape=(
            jax.ShapeDtypeStruct((2, RADIX, RADIX), F32),
            jax.ShapeDtypeStruct((8, RADIX), F32),
        ),
        compiler_params=params,
        name="window_spectra",
    )(gated, prev, th, tl, tables[2], fu)
    return pl.pallas_call(
        inverse_kernel,
        out_shape=jax.ShapeDtypeStruct((template_total, RADIX), F32),
        grid=(template_total,),
        in_specs=[
            pl.BlockSpec((1, 2, HALF, RADIX), lambda k: (k, 0, 0, 0)),
            whole((2, RADIX, RADIX)),
            whole((8, RADIX)),
            *(whole(t.shape) for t in tables),
        ],
        out_specs=whole((template_total, RADIX)),
        scratch_shapes=[pltpu.VMEM((2 * RADIX, 2 * RADIX), F32), pltpu.VMEM((1, RADIX), F32)],
        compiler_params=params,
        name="series_peaks",
    )(bank, spectra, gain, *tables)


def solution(mesh):
    in_specs = (P(("grp", "seg")), P(("grp", "seg")), P("grp", None, "seg"))
    out_specs = P(None, ("grp", "seg"))
    return jax.shard_map(local, mesh=mesh, in_specs=in_specs, out_specs=out_specs, check_vma=False)
```

time: 41.9 us -> 36.7 us (0.88)
  Pallas kernels: 38.7 us -> 33.3 us
    pallas_call x1, Pallas kernels: 38.7 us -> 33.3 us  [fused(): pl.pallas_call(fused_kernel, out_shape=jax.ShapeDtypeStruct((template_tot...]
where the time goes in v4:
time: 36.7 us; the launch traced here: 36.3 us
  Pallas kernels  33.3 us (91%)
  local copies, waits for them, and re-layouts  2.95 us (8%)
    pallas_call x1, Pallas kernels, fused(): pl.pallas_call(fused_kernel, out_shape=jax.ShapeDtypeStruct((template_tot...  33.3 us
    reshape x1, local copies, waits for them, and re-layouts, local(): template_bank.reshape(template_total, -1, RADIX)  1.63 us
    unnamed x1, local copies, waits for them, and re-layouts  1.32 us

profile of v4, /device:TPU:0, one launch (start us, length us, event | category | flops | bytes accessed | tf_op | source)
XLA Modules:
  0.0 36.3 jit_solution(13027222517914633167)
XLA Ops:
  0.0 1.6 %reshape.11.bank_ref = bf16[16,16,256]{2,1,0:T(8,128)(2,1)} reshape(bf16[16,2,2048]{2,1,0:T(2,128)(2,1)} %param.13) | data formatting | bytes 262144 | tf_op jit(solution)/shard_map/reshape | solution.py:391
  1.6 33.3 %matched_filter.1 = f32[16,256]{1,0:T(8,128)} custom-call(f32[512,128]{1,0:T(8,128)} %bitcast.2, s32[512,128]{1,0:T(8,128)} %bitcast.3, bf16[16,16,256]{2,1,0:T(8,128)(2,1)} %reshape.11.bank_ref, bf16[128,512]{1,0:T(8,128)(2,1)} %constant.16.clone.refs_0_, bf16[128,512]{1,0:T(8,128)(2,1)} %constant.17.clone.refs_1_, ...), custom_call_target="tpu_custom_call" | custom-call | tf_op jit(solution)/shard_map/matched_filter/pallas_call | solution.py:352
  34.9 1.3 %copy.13 = f32[16,256]{1,0:T(8,128)} copy(f32[16,256]{1,0:T(8,128)} %matched_filter.1) | data formatting | bytes 32768

commit v5 on v4

--- a/solution.py
+++ b/solution.py
@@ -21,6 +21,7 @@
 NARROW = 16.0
 SHRINK = 128.0
 TOP = 16.0
+ROWS = 32
 MESH = pl.DeviceIdType.MESH
 VMEM_LIMIT = 56 * 1024 * 1024
 SEGS = 16
@@ -28,6 +29,7 @@
 GROUPS = 4
 CHIPS = 8
 TABLES = 8
+WORK = 5
 
 
 def angles(rows, cols, period):
@@ -85,55 +87,96 @@
     return jnp.dot(left, right, preferred_element_type=F32)
 
 
-def inverse_kernel(h_ref, x_ref, gain_ref, t_ref, tr_ref, w_ref, u_ref, ur_ref, o_ref, part_ref, scale_ref):
+def inverse_kernel(
+    h_ref, x_ref, gain_ref, t_ref, tr_ref, w_ref, u_ref, ur_ref, o_ref, part_ref, scale_ref, *work
+):
+    def bank_tile(row, lane):
+        spot = (pl.ds(row, ROWS), pl.ds(lane, 128))
+        return h_ref[0, 0, *spot].astype(F32), h_ref[0, 1, *spot].astype(F32)
+
+    def window_tile(block, row, lane):
+        return x_ref[block, pl.ds(row, ROWS), pl.ds(lane, 128)]
+
     index = pl.program_id(0)
-    bank_real, bank_imag = h_ref[0, 0].astype(F32), h_ref[0, 1].astype(F32)
-    windows = [(x_ref[block, :HALF], x_ref[block, HALF:]) for block in range(2)]
-    first_product(bank_real, bank_imag, windows, t_ref, tr_ref, part_ref, scale_ref)
-    peaks = second_product(part_ref, scale_ref, gain_ref[:1], w_ref, u_ref, ur_ref)
+    first_product(bank_tile, window_tile, t_ref, tr_ref, part_ref, scale_ref, work)
+    peaks = second_product(part_ref, scale_ref, gain_ref[:1], w_ref, u_ref, ur_ref, work)
     row = lax.broadcasted_iota(jnp.int32, o_ref.shape, 0)
     o_ref[...] = jnp.where(row == index, peaks, o_ref[...])
 
 
-def first_product(bank_real, bank_imag, windows, t_ref, tr_ref, part_ref, scale_ref):
-    scale = 1.0 / (BLOCK * jnp.sum(bank_real * bank_real + bank_imag * bank_imag) + EPSILON)
+TILES = [(row, lane) for row in range(0, RADIX, ROWS) for lane in range(0, RADIX, 128)]
+
+
+def first_product(bank_tile, window_tile, t_ref, tr_ref, part_ref, scale_ref, work):
+    high_ref, rest_ref = work[:2]
+    total = jnp.zeros((8, 128), F32)
+    for row, lane in TILES:
+        if row >= HALF:
+            continue
+        bank_real, bank_imag = bank_tile(row, lane)
+        power = bank_real * bank_real + bank_imag * bank_imag
+        total = total + jnp.sum(power.reshape(ROWS // 8, 8, 128), axis=0)
+        for block in range(2):
+            real, imag = window_tile(block, row, lane), window_tile(block, row + HALF, lane)
+            columns = pl.ds(block * RADIX + lane, 128)
+            values = (real * bank_real + imag * bank_imag, imag * bank_real - real * bank_imag)
+            for at, value in zip((row, row + HALF), values):
+                high, rest, value = split_small(value)
+                high_ref[pl.ds(at, ROWS), columns] = high
+                rest_ref[pl.ds(at, ROWS), columns] = rest
+                rest_ref[pl.ds(at + RADIX, ROWS), columns] = value
+    scale = 1.0 / (BLOCK * jnp.sum(total) + EPSILON)
     scale_ref[...] = jnp.full(scale_ref.shape, scale, F32)
-    pieces = []
-    for real, imag in windows:
-        pieces.append(
-            split_small(
-                jnp.concatenate(
-                    [real * bank_real + imag * bank_imag, imag * bank_real - real * bank_imag],
-                    axis=0,
-                )
+    part_ref[0] = dot(t_ref[...], high_ref[...])
+    part_ref[1] = dot(tr_ref[...], rest_ref[...])
+
+
+def second_product(part_ref, scale_ref, gain, w_ref, u_ref, ur_ref, work):
+    high_ref, rest_ref, series_ref = work[2:]
+    for row, lane in TILES:
+        spot = (pl.ds(row, ROWS), pl.ds(lane, 128))
+        cos = w_ref[0, *spot] * (1.0 / (LIFT * SHRINK))
+        sin = w_ref[1, *spot] * (1.0 / (LIFT * SHRINK))
+        for block in range(2):
+            columns = pl.ds(block * RADIX + lane, 128)
+            real, imag = (
+                part_ref[0, pl.ds(at, ROWS), columns] + part_ref[1, pl.ds(at, ROWS), columns]
+                for at in (row, row + RADIX)
             )
-        )
-    high, rest, value = (jnp.concatenate(pair, axis=1) for pair in zip(*pieces))
-    part_ref[...] = dot(t_ref[...], high) + dot(
-        tr_ref[...], jnp.concatenate([rest, value], axis=0)
-    )
-
-
-def second_product(part_ref, scale_ref, gain, w_ref, u_ref, ur_ref):
-    cos, sin = w_ref[0] * (1.0 / (LIFT * SHRINK)), w_ref[1] * (1.0 / (LIFT * SHRINK))
-    pieces = []
+            rows = pl.ds(block * RADIX + row, ROWS)
+            values = (real * cos - imag * sin, real * sin + imag * cos)
+            for at, value in zip((lane, lane + RADIX), values):
+                high, rest, value = split_small(value)
+                high_ref[rows, pl.ds(at, 128)] = high
+                rest_ref[rows, pl.ds(at, 128)] = rest
+                rest_ref[rows, pl.ds(at + 2 * RADIX, 128)] = value
+    series_ref[0] = dot(high_ref[...], u_ref[...])
+    series_ref[1] = dot(rest_ref[...], ur_ref[...])
+    peaks = []
     for block in range(2):
-        columns = slice(block * RADIX, (block + 1) * RADIX)
-        real, imag = part_ref[:RADIX, columns], part_ref[RADIX:, columns]
-        high, rest, value = split_small(
-            jnp.concatenate([real * cos - imag * sin, real * sin + imag * cos], axis=1)
-        )
-        pieces.append((high, jnp.concatenate([rest, value], axis=1)))
-    high, small_parts = (jnp.concatenate(pair, axis=0) for pair in zip(*pieces))
-    series = dot(high, u_ref[...]) + dot(small_parts, ur_ref[...])
-    real, imag = series[:, :HALF], series[:, HALF:]
-    power = real * real + imag * imag
-    peaks = [
-        jnp.max(power[block * RADIX : (block + 1) * RADIX], axis=0, keepdims=True)
-        for block in range(2)
-    ]
+        best = jnp.zeros((8, HALF), F32)
+        for row in range(block * RADIX, (block + 1) * RADIX, ROWS):
+            series = series_ref[0, pl.ds(row, ROWS)] + series_ref[1, pl.ds(row, ROWS)]
+            real, imag = series[:, :HALF], series[:, HALF:]
+            power = (real * real + imag * imag).reshape(ROWS // 8, 8, HALF)
+            best = jnp.maximum(best, jnp.max(power, axis=0))
+        peaks.append(jnp.max(best, axis=0, keepdims=True))
     both = jnp.concatenate(peaks, axis=1) * ((SHRINK / LIFT) ** 2 * scale_ref[...])
     return both * gain * gain
+
+
+def part_scratch():
+    return pltpu.VMEM((2, 2 * RADIX, 2 * RADIX), F32)
+
+
+def work_scratch():
+    return [
+        pltpu.VMEM((RADIX, 2 * RADIX), BF16),
+        pltpu.VMEM((2 * RADIX, 2 * RADIX), F8),
+        pltpu.VMEM((2 * RADIX, 2 * RADIX), BF16),
+        pltpu.VMEM((2 * RADIX, 4 * RADIX), F8),
+        pltpu.VMEM((2, 2 * RADIX, RADIX), F32),
+    ]
 
 
 def window_spectra(grids, th_ref, tl_ref, w_ref, u_ref):
@@ -173,6 +216,7 @@
 def fused_kernel(strain_ref, mask_ref, bank_ref, *refs):
     outside, refs = refs[:TABLES], refs[TABLES:]
     o_ref, gated, prev, held, x_ref, peak_ref, got_ref, part_a, part_b, scale_a, scale_b, *refs = refs
+    work_a, work_b, refs = refs[:WORK], refs[WORK : 2 * WORK], refs[2 * WORK :]
     prev_sem, swap_send, swap_recv, own_send, pass_send, recv_sem, side_sem, table_sem, *tables = refs
     th_ref, tl_ref, fu_ref, t_ref, tr_ref, w_ref, u_ref, ur_ref = tables
     me = lax.axis_index("seg")
@@ -290,18 +334,22 @@
     own(3)
 
     def first(template, side, part_ref, scale_ref):
-        rows = held[:, template].astype(F32).reshape(SEGS, -1, RADIX)
-        half = rows.shape[1] // 2
-        bank_real = rows[:, :half].reshape(HALF, RADIX)
-        bank_imag = rows[:, half:].reshape(HALF, RADIX)
-        windows = [
-            (x_ref[side, at : at + HALF], x_ref[side, at + HALF : at + RADIX]) for at in (0, RADIX)
-        ]
-        first_product(bank_real, bank_imag, windows, t_ref, tr_ref, part_ref, scale_ref)
+        def bank_tile(row, lane):
+            chips = pl.ds(row // 16, ROWS // 16)
+            rows = held[chips, template, :, :, pl.ds(lane, 128)].astype(F32)
+            real, imag = rows[:, :, :8], rows[:, :, 8:]
+            return real.reshape(ROWS, 128), imag.reshape(ROWS, 128)
+
+        def window_tile(block, row, lane):
+            return x_ref[side, pl.ds(block * RADIX + row, ROWS), pl.ds(lane, 128)]
+
+        work = work_b if side else work_a
+        first_product(bank_tile, window_tile, t_ref, tr_ref, part_ref, scale_ref, work)
 
     def second(template, side, part_ref, scale_ref):
         gain = x_ref[side, 2 * RADIX : 2 * RADIX + 1]
-        peaks = second_product(part_ref, scale_ref, gain, w_ref, u_ref, ur_ref)
+        work = work_b if side else work_a
+        peaks = second_product(part_ref, scale_ref, gain, w_ref, u_ref, ur_ref, work)
         row = lax.broadcasted_iota(jnp.int32, got_ref.shape, 0)
         peak_ref[side] = jnp.where(row == template, peaks, peak_ref[side])
 
@@ -361,8 +409,10 @@
             pltpu.VMEM((2, 2 * RADIX + 8, RADIX), F32),
             pltpu.VMEM((2, template_total // 2, RADIX), F32),
             pltpu.VMEM((template_total // 2, RADIX), F32),
-            *[pltpu.VMEM((2 * RADIX, 2 * RADIX), F32)] * 2,
+            *[part_scratch()] * 2,
             *[pltpu.VMEM((1, RADIX), F32)] * 2,
+            *work_scratch(),
+            *work_scratch(),
             pltpu.SemaphoreType.DMA((2,)),
             pltpu.SemaphoreType.DMA((GROUPS,)),
             pltpu.SemaphoreType.DMA((GROUPS,)),
@@ -417,7 +467,7 @@
             *(whole(t.shape) for t in tables),
         ],
         out_specs=whole((template_total, RADIX)),
-        scratch_shapes=[pltpu.VMEM((2 * RADIX, 2 * RADIX), F32), pltpu.VMEM((1, RADIX), F32)],
+        scratch_shapes=[part_scratch(), pltpu.VMEM((1, RADIX), F32), *work_scratch()],
         compiler_params=params,
         name="series_peaks",
     )(bank, spectra, gain, *tables)

time: 36.7 us -> 38.2 us (1.041)
  Pallas kernels: 33.3 us -> 35 us
    pallas_call x1, Pallas kernels: 33.3 us -> 35 us  [fused(): pl.pallas_call(fused_kernel, out_shape=jax.ShapeDtypeStruct((template_tot...]
where the time goes in v5:
time: 38.2 us; the launch traced here: 37.9 us
  Pallas kernels  35 us (92%)
  local copies, waits for them, and re-layouts  2.95 us (8%)
    pallas_call x1, Pallas kernels, fused(): pl.pallas_call(fused_kernel, out_shape=jax.ShapeDtypeStruct((template_tot...  35 us
    reshape x1, local copies, waits for them, and re-layouts, local(): template_bank.reshape(template_total, -1, RADIX)  1.63 us
    unnamed x1, local copies, waits for them, and re-layouts  1.32 us

profile of v5, /device:TPU:0, one launch (start us, length us, event | category | flops | bytes accessed | tf_op | source)
XLA Modules:
  0.0 37.9 jit_solution(5911151146542686551)
XLA Ops:
  0.0 1.6 %reshape.11.bank_ref = bf16[16,16,256]{2,1,0:T(8,128)(2,1)} reshape(bf16[16,2,2048]{2,1,0:T(2,128)(2,1)} %param.13) | data formatting | bytes 262144 | tf_op jit(solution)/shard_map/reshape | solution.py:441
  1.6 35.0 %matched_filter.1 = f32[16,256]{1,0:T(8,128)} custom-call(f32[512,128]{1,0:T(8,128)} %bitcast.2, s32[512,128]{1,0:T(8,128)} %bitcast.3, bf16[16,16,256]{2,1,0:T(8,128)(2,1)} %reshape.11.bank_ref, bf16[128,512]{1,0:T(8,128)(2,1)} %constant.16.clone.refs_0_, bf16[128,512]{1,0:T(8,128)(2,1)} %constant.17.clone.refs_1_, ...), custom_call_target="tpu_custom_call" | custom-call | tf_op jit(solution)/shard_map/matched_filter/pallas_call | solution.py:400
  36.6 1.3 %copy.13 = f32[16,256]{1,0:T(8,128)} copy(f32[16,256]{1,0:T(8,128)} %matched_filter.1) | data formatting | bytes 32768
